TPU v7x, 256 devices: a whole 4x4x8 slice. The times are simulated.
256 devices in a mesh: span: 32 (over y, z), tp: 8 (over x, core).
Axes of the slice: x: 4, y: 4, z: 8, core: 2. Of those that a mesh axis runs over, the one named last changes fastest.
Arguments:
- latent: bfloat16 [16384, 5120], P(('span', 'tp')), may hold values from -6 to 6
- queries: bfloat16 [16384, 5120], P('span', 'tp'), may hold values from -8 to 8
- keys: bfloat16 [16384, 5120], P('span', 'tp'), may hold values from -8 to 8
- values: bfloat16 [16384, 5120], P('span', 'tp'), may hold values from -6 to 6
- out_weight: bfloat16 [5120, 5120], P('tp'), may hold values from -0.078125 to 0.078125
- level_gate: float32 [4, 5120], replicated, may hold values from 1 to 4
- levels: int32 [32], P('span'), may hold values from 0 to 3
- offset: int32 [1], replicated, may hold values from 0 to 31
- lag_mask: int32 [32, 7], P('span'), may hold values 0 or 1
- fresh_noise: bfloat16 [512, 5120], P('tp'), may hold values from -6 to 6
Outputs:
- next_latent: bfloat16 [16384, 5120], P(('span', 'tp'))
- released: bfloat16 [512, 5120], P('tp', 'span')
All inputs are finite; a program needn't handle non-finite values. No bound on the sum of `lag_mask` on one device may be relied on, other than what follows from the above.
Results may differ from a plain program's by a relative error of at most 0.012.
Values may be sent and summed in bfloat16 or wider, within the bound.
A program may use at most 128 MiB of HBM per device.

v0:
```python
import jax
import jax.numpy as jnp
from jax import lax
from jax.sharding import PartitionSpec as P

HEAD_DIM = 128
LEVELS = 4


def from_behind(block, axis, distance):
    devices = range(lax.axis_size(axis))
    route = [((i - distance) % len(devices), i) for i in devices]
    return lax.ppermute(block, axis, route)


def from_root(value, axis, source):
    kept = jnp.where(lax.axis_index(axis) == source, value, 0).astype(value.dtype)
    return lax.psum(kept, axis)


def body(
    latent, queries, keys, values, out_weight, level_gate, levels, offset, lag_mask, fresh_noise
):
    slot_count = lax.axis_size("span")
    my_slot = lax.axis_index("span")
    position = (my_slot - offset[0]) % slot_count
    row_count, feat_width = queries.shape
    head_count = feat_width // HEAD_DIM
    lag_count = lag_mask.shape[1]
    block_count = lag_count + 1
    score_scale = HEAD_DIM ** (-0.5)
    blocks = [(keys, values)]
    for lag_index in range(1, lag_count + 1):
        blocks.append(from_behind((keys, values), "span", lag_index))
    lag_steps = jnp.arange(1, lag_count + 1, dtype=jnp.int32)
    usable = jnp.concatenate(
        [jnp.ones((1,), jnp.bool_), (lag_mask[0] == 1) & (position >= lag_steps)]
    )
    key_stack = (
        jnp.stack([pair[0] for pair in blocks])
        .reshape(block_count, row_count, head_count, HEAD_DIM)
        .transpose(2, 0, 1, 3)
    )
    value_stack = (
        jnp.stack([pair[1] for pair in blocks])
        .reshape(block_count, row_count, head_count, HEAD_DIM)
        .transpose(2, 0, 1, 3)
    )
    query_heads = queries.reshape(row_count, head_count, HEAD_DIM).transpose(1, 0, 2)

    def one_head(operands):
        query, key_blocks, value_blocks = operands
        scores = (
            jnp.einsum("qd,lkd->lqk", query, key_blocks, preferred_element_type=jnp.float32)
            * score_scale
        )
        scores = jnp.where(usable[:, None, None], scores, -jnp.inf)
        row_peak = jnp.max(scores, axis=(0, 2))
        weights = jnp.exp(scores - row_peak[None, :, None])
        row_total = jnp.sum(weights, axis=(0, 2))
        weighted = jnp.einsum(
            "lqk,lkd->qd",
            weights.astype(jnp.bfloat16),
            value_blocks,
            preferred_element_type=jnp.float32,
        )
        return (weighted / row_total[:, None]).astype(jnp.bfloat16)

    attended = lax.map(one_head, (query_heads, key_stack, value_stack))
    attended = attended.transpose(1, 0, 2).reshape(row_count, feat_width)
    summed = lax.psum_scatter(
        jnp.dot(attended, out_weight, preferred_element_type=jnp.float32).astype(jnp.bfloat16),
        "tp",
        scatter_dimension=0,
        tiled=True,
    ).astype(jnp.float32)
    gate_row = lax.dynamic_index_in_dim(level_gate, levels[0], 0, keepdims=False)
    updated = (latent.astype(jnp.float32) - gate_row[None, :] * summed / LEVELS).astype(
        jnp.bfloat16
    )
    oldest_rows = from_root(updated, "span", offset[0])
    share_width = oldest_rows.shape[1] // slot_count
    released = lax.dynamic_slice_in_dim(oldest_rows, my_slot * share_width, share_width, 1)
    next_latent = jnp.where(position == 0, fresh_noise, updated)
    return (next_latent, released)


def solution(mesh):
    return jax.shard_map(
        body,
        mesh=mesh,
        in_specs=(
            P(("span", "tp"), None),
            P("span", "tp"),
            P("span", "tp"),
            P("span", "tp"),
            P("tp", None),
            P(),
            P("span"),
            P(),
            P("span", None),
            P("tp", None),
        ),
        out_specs=(P(("span", "tp"), None), P("tp", "span")),
        check_vma=False,
    )
```

profile of v0, /device:TPU:2, one launch (start us, length us, event | category | flops | bytes accessed | tf_op | source)
XLA Modules:
  0.0 526.3 jit_solution(4812700630474028496)
XLA Ops:
  10.6 3.3 collective-permute-start.8
  13.9 4.0 collective-permute-start.9
  19.5 4.9 collective-permute-start.11
  28.0 5.0 collective-permute-done.7
  33.1 9.4 %collective-permute-start.12 = (bf16[512,640]{0,1:T(8,128)(2,1)S(1)}, bf16[512,640]{0,1:T(8,128)(2,1)}, u32[]{:S(2)}, u32[]{:S(2)}) collective-permute-start(bf16[512,640]{0,1:T(8,128)(2,1)S(1)} %copy.23), channel_id=1, source_target_pairs={{208,0},{216,8},{224,16},{232,24},{240,32},{248,40},{0,48},{8,56},... | collective-permute-start | bytes 1966088 | tf_op jit(solution)/shard_map/ppermute | solution.py:13
  43.3 20.4 %collective-permute-done.8 = bf16[512,640]{0,1:T(8,128)(2,1)S(1)} collective-permute-done((bf16[512,640]{0,1:T(8,128)(2,1)S(1)}, bf16[512,640]{0,1:T(8,128)(2,1)S(1)}, u32[]{:S(2)}, u32[]{:S(2)}) %collective-permute-start.8) | collective-permute-done | bytes 655392 | tf_op jit(solution)/shard_map/ppermute | solution.py:13
  63.7 3.5 collective-permute-start.13
  67.6 68.5 %collective-permute-done.9 = bf16[512,640]{0,1:T(8,128)(2,1)} collective-permute-done((bf16[512,640]{0,1:T(8,128)(2,1)S(1)}, bf16[512,640]{0,1:T(8,128)(2,1)}, u32[]{:S(2)}, u32[]{:S(2)}) %collective-permute-start.9) | collective-permute-done | bytes 655392 | tf_op jit(solution)/shard_map/ppermute | solution.py:13
  138.1 8.1 %collective-permute-start.1 = (bf16[512,640]{0,1:T(8,128)(2,1)S(1)}, bf16[512,640]{0,1:T(8,128)(2,1)S(1)}, u32[]{:S(2)}, u32[]{:S(2)}) collective-permute-start(bf16[512,640]{0,1:T(8,128)(2,1)S(1)} %copy.14), channel_id=1, source_target_pairs={{240,0},{248,8},{0,16},{8,24},{16,32},{24,40},{32,48},{40,56},{48,... | collective-permute-start | bytes 1966088 | tf_op jit(solution)/shard_map/ppermute | solution.py:13
  153.2 3.0 collective-permute-done.13
  159.0 7.2 %collective-permute-done = bf16[512,640]{0,1:T(8,128)(2,1)S(1)} collective-permute-done((bf16[512,640]{0,1:T(8,128)(2,1)S(1)}, bf16[512,640]{0,1:T(8,128)(2,1)S(1)}, u32[]{:S(2)}, u32[]{:S(2)}) %collective-permute-start) | collective-permute-done | bytes 655392 | tf_op jit(solution)/shard_map/ppermute | solution.py:13
  168.3 24.8 %collective-permute-done.1 = bf16[512,640]{0,1:T(8,128)(2,1)S(1)} collective-permute-done((bf16[512,640]{0,1:T(8,128)(2,1)S(1)}, bf16[512,640]{0,1:T(8,128)(2,1)S(1)}, u32[]{:S(2)}, u32[]{:S(2)}) %collective-permute-start.1) | collective-permute-done | bytes 655392 | tf_op jit(solution)/shard_map/ppermute | solution.py:13
  196.0 55.2 %collective-permute-done.2 = bf16[512,640]{0,1:T(8,128)(2,1)S(1)} collective-permute-done((bf16[512,640]{0,1:T(8,128)(2,1)S(1)}, bf16[512,640]{0,1:T(8,128)(2,1)S(1)}, u32[]{:S(2)}, u32[]{:S(2)}) %collective-permute-start.2) | collective-permute-done | bytes 655392 | tf_op jit(solution)/shard_map/ppermute | solution.py:13
  251.4 3.1 collective-permute-done.5
  254.5 15.4 %collective-permute-done.6 = bf16[512,640]{0,1:T(8,128)(2,1)S(1)} collective-permute-done((bf16[512,640]{0,1:T(8,128)(2,1)S(1)}, bf16[512,640]{0,1:T(8,128)(2,1)S(1)}, u32[]{:S(2)}, u32[]{:S(2)}) %collective-permute-start.6) | collective-permute-done | bytes 655392 | tf_op jit(solution)/shard_map/ppermute | solution.py:13
  272.3 38.8 %while.10 = (s32[]{:T(128)}, bf16[5,512,128]{1,2,0:T(8,128)(2,1)S(1)}, pred[8]{0:T(512)(128)(4,1)S(1)}, bf16[5,8,512,128]{2,3,0,1:T(8,128)(2,1)}, bf16[5,512,128...) while((s32[]{:T(128)}, bf16[5,512,128]{1,2,0:T(8,128)(2,1)S(1)}, ...), condition=%wide.region_3.4_spmd, body=%wide.region_0.3_spmd.sunk | while | flops 1096940544 | bytes 28061792 | solution.py:69
  276.7 3.2 fusion.41
  284.4 3.2 fusion.41
  292.2 3.2 fusion.41
  300.0 3.2 fusion.41
  307.8 3.2 fusion.41
  311.2 8.9 %convolution_convert_fusion = bf16[512,5120]{1,0:T(8,128)(2,1)} fusion(bf16[512,640]{0,1:T(8,128)(2,1)S(1)} %bitcast.101, bf16[640,5120]{1,0:T(8,128)(2,1)} %param.16), kind=kOutput, calls=%fused_computation.24 | convolution fusion | flops 3358064640 | bytes 12451840 | tf_op jit(solution)/shard_map/dot_general | solution.py:72
  320.9 42.1 %reduce-scatter.2.cloned.1.call-done = bf16[64,5120]{1,0:T(8,128)(2,1)} async-done(((bf16[512,5120]{1,0:T(8,128)(2,1)}), bf16[64,5120]{1,0:T(8,128)(2,1)}) %reduce-scatter.2.cloned.1.call-update) | async-done | bytes 655376 | tf_op jit(solution)/shard_map/reduce_scatter | solution.py:71
  365.6 152.3 %all-reduce.2.cloned.1.call-done = bf16[64,5120]{1,0:T(8,128)(2,1)} async-done(((bf16[64,5120]{1,0:T(8,128)(2,1)}), bf16[64,5120]{1,0:T(8,128)(2,1)}) %all-reduce.2.cloned.1.call-update) | async-done | bytes 655376 | tf_op jit(solution)/shard_map/psum | solution.py:18
  (78 shorter events, 55.1 us)
Async XLA Ops:
  7.2 313.7 %copy-start = (f32[4,5120]{1,0:T(4,128)S(1)}, f32[4,5120]{1,0:T(4,128)}, u32[]{:S(2)}) copy-start(f32[4,5120]{1,0:T(4,128)} %param.17) | copy-start | bytes 245764
  7.2 60.1 %copy-start.3 = (bf16[512,640]{1,0:T(8,128)(2,1)S(1)}, bf16[512,640]{1,0:T(8,128)(2,1)}, u32[]{:S(2)}) copy-start(bf16[512,640]{1,0:T(8,128)(2,1)} %param.13) | copy-start | bytes 1966084
  7.2 355.8 %reduce-scatter.2.cloned.1.call-start = ((), (), s32[]{:S(2)}) async-start(), calls=%async_computation.1 | async-start | bytes 5898240 | tf_op jit(solution)/shard_map/reduce_scatter | solution.py:71
  8.6 24.4 %collective-permute-start.7 = (bf16[512,640]{0,1:T(8,128)(2,1)S(1)}, bf16[512,640]{0,1:T(8,128)(2,1)S(1)}, u32[]{:S(2)}, u32[]{:S(2)}) collective-permute-start(bf16[512,640]{0,1:T(8,128)(2,1)S(1)} %copy.23), channel_id=1, source_target_pairs={{248,0},{0,8},{8,16},{16,24},{24,32},{32,40},{40,48},{48,56},{56,6... | collective-permute-start | bytes 1966088 | tf_op jit(solution)/shard_map/ppermute | solution.py:13
  10.6 53.1 %collective-permute-start.8 = (bf16[512,640]{0,1:T(8,128)(2,1)S(1)}, bf16[512,640]{0,1:T(8,128)(2,1)S(1)}, u32[]{:S(2)}, u32[]{:S(2)}) collective-permute-start(bf16[512,640]{0,1:T(8,128)(2,1)S(1)} %copy.23), channel_id=1, source_target_pairs={{240,0},{248,8},{0,16},{8,24},{16,32},{24,40},{32,48},{40,56},{48,... | collective-permute-start | bytes 1966088 | tf_op jit(solution)/shard_map/ppermute | solution.py:13
  13.9 122.2 %collective-permute-start.9 = (bf16[512,640]{0,1:T(8,128)(2,1)S(1)}, bf16[512,640]{0,1:T(8,128)(2,1)}, u32[]{:S(2)}, u32[]{:S(2)}) collective-permute-start(bf16[512,640]{0,1:T(8,128)(2,1)S(1)} %copy.23), channel_id=1, source_target_pairs={{232,0},{240,8},{248,16},{0,24},{8,32},{16,40},{24,48},{32,56},{40... | collective-permute-start | bytes 1966088 | tf_op jit(solution)/shard_map/ppermute | solution.py:13
  17.9 120.1 %collective-permute-start.10 = (bf16[512,640]{0,1:T(8,128)(2,1)S(1)}, bf16[512,640]{0,1:T(8,128)(2,1)}, u32[]{:S(2)}, u32[]{:S(2)}) collective-permute-start(bf16[512,640]{0,1:T(8,128)(2,1)S(1)} %copy.23), channel_id=1, source_target_pairs={{224,0},{232,8},{240,16},{248,24},{0,32},{8,40},{16,48},{24,56},{3... | collective-permute-start | bytes 1966088 | tf_op jit(solution)/shard_map/ppermute | solution.py:13
  19.5 129.6 %collective-permute-start.11 = (bf16[512,640]{0,1:T(8,128)(2,1)S(1)}, bf16[512,640]{0,1:T(8,128)(2,1)}, u32[]{:S(2)}, u32[]{:S(2)}) collective-permute-start(bf16[512,640]{0,1:T(8,128)(2,1)S(1)} %copy.23), channel_id=1, source_target_pairs={{216,0},{224,8},{232,16},{240,24},{248,32},{0,40},{8,48},{16,56},{... | collective-permute-start | bytes 1966088 | tf_op jit(solution)/shard_map/ppermute | solution.py:13
  33.1 34.2 %copy-start.4 = (bf16[512,640]{0,1:T(8,128)(2,1)}, bf16[512,640]{0,1:T(8,128)(2,1)S(1)}, u32[]{:S(2)}) copy-start(bf16[512,640]{0,1:T(8,128)(2,1)S(1)} %collective-permute-done.7) | copy-start | bytes 1966084
  33.1 118.1 %collective-permute-start.12 = (bf16[512,640]{0,1:T(8,128)(2,1)S(1)}, bf16[512,640]{0,1:T(8,128)(2,1)}, u32[]{:S(2)}, u32[]{:S(2)}) collective-permute-start(bf16[512,640]{0,1:T(8,128)(2,1)S(1)} %copy.23), channel_id=1, source_target_pairs={{208,0},{216,8},{224,16},{232,24},{240,32},{248,40},{0,48},{8,56},... | collective-permute-start | bytes 1966088 | tf_op jit(solution)/shard_map/ppermute | solution.py:13
  63.7 92.6 %collective-permute-start.13 = (bf16[512,640]{0,1:T(8,128)(2,1)S(1)}, bf16[512,640]{0,1:T(8,128)(2,1)}, u32[]{:S(2)}, u32[]{:S(2)}) collective-permute-start(bf16[512,640]{0,1:T(8,128)(2,1)S(1)} %copy.23), channel_id=1, source_target_pairs={{200,0},{208,8},{216,16},{224,24},{232,32},{240,40},{248,48},{0,56... | collective-permute-start | bytes 1966088 | tf_op jit(solution)/shard_map/ppermute | solution.py:13
  67.5 128.4 %copy-start.1 = (bf16[8,512,5,128]{1,3,2,0:T(8,128)(2,1)S(1)}, bf16[8,512,5,128]{1,3,2,0:T(8,128)(2,1)}, u32[]{:S(2)}) copy-start(bf16[8,512,5,128]{1,3,2,0:T(8,128)(2,1)} %constant_dynamic-update-slice_fusion.8) | copy-start | bytes 15728644
  136.1 30.1 %collective-permute-start = (bf16[512,640]{0,1:T(8,128)(2,1)S(1)}, bf16[512,640]{0,1:T(8,128)(2,1)S(1)}, u32[]{:S(2)}, u32[]{:S(2)}) collective-permute-start(bf16[512,640]{0,1:T(8,128)(2,1)S(1)} %copy.14), channel_id=1, source_target_pairs={{248,0},{0,8},{8,16},{16,24},{24,32},{32,40},{40,48},{48,56},{56,6... | collective-permute-start | bytes 1966088 | tf_op jit(solution)/shard_map/ppermute | solution.py:13
  138.1 55.0 %collective-permute-start.1 = (bf16[512,640]{0,1:T(8,128)(2,1)S(1)}, bf16[512,640]{0,1:T(8,128)(2,1)S(1)}, u32[]{:S(2)}, u32[]{:S(2)}) collective-permute-start(bf16[512,640]{0,1:T(8,128)(2,1)S(1)} %copy.14), channel_id=1, source_target_pairs={{240,0},{248,8},{0,16},{8,24},{16,32},{24,40},{32,48},{40,56},{48,... | collective-permute-start | bytes 1966088 | tf_op jit(solution)/shard_map/ppermute | solution.py:13
  149.1 102.1 %collective-permute-start.2 = (bf16[512,640]{0,1:T(8,128)(2,1)S(1)}, bf16[512,640]{0,1:T(8,128)(2,1)S(1)}, u32[]{:S(2)}, u32[]{:S(2)}) collective-permute-start(bf16[512,640]{0,1:T(8,128)(2,1)S(1)} %copy.14), channel_id=1, source_target_pairs={{232,0},{240,8},{248,16},{0,24},{8,32},{16,40},{24,48},{32,56},{40... | collective-permute-start | bytes 1966088 | tf_op jit(solution)/shard_map/ppermute | solution.py:13
  151.1 100.1 %collective-permute-start.3 = (bf16[512,640]{0,1:T(8,128)(2,1)S(1)}, bf16[512,640]{0,1:T(8,128)(2,1)S(1)}, u32[]{:S(2)}, u32[]{:S(2)}) collective-permute-start(bf16[512,640]{0,1:T(8,128)(2,1)S(1)} %copy.14), channel_id=1, source_target_pairs={{224,0},{232,8},{240,16},{248,24},{0,32},{8,40},{16,48},{24,56},{3... | collective-permute-start | bytes 1966088 | tf_op jit(solution)/shard_map/ppermute | solution.py:13
  156.3 95.1 %collective-permute-start.4 = (bf16[512,640]{0,1:T(8,128)(2,1)S(1)}, bf16[512,640]{0,1:T(8,128)(2,1)S(1)}, u32[]{:S(2)}, u32[]{:S(2)}) collective-permute-start(bf16[512,640]{0,1:T(8,128)(2,1)S(1)} %copy.14), channel_id=1, source_target_pairs={{216,0},{224,8},{232,16},{240,24},{248,32},{0,40},{8,48},{16,56},{... | collective-permute-start | bytes 1966088 | tf_op jit(solution)/shard_map/ppermute | solution.py:13
  166.2 88.3 %collective-permute-start.5 = (bf16[512,640]{0,1:T(8,128)(2,1)S(1)}, bf16[512,640]{0,1:T(8,128)(2,1)S(1)}, u32[]{:S(2)}, u32[]{:S(2)}) collective-permute-start(bf16[512,640]{0,1:T(8,128)(2,1)S(1)} %copy.14), channel_id=1, source_target_pairs={{208,0},{216,8},{224,16},{232,24},{240,32},{248,40},{0,48},{8,56},... | collective-permute-start | bytes 1966088 | tf_op jit(solution)/shard_map/ppermute | solution.py:13
  166.2 106.1 %copy-start.7 = (bf16[5,512,128]{1,2,0:T(8,128)(2,1)S(1)}, bf16[5,512,128]{1,2,0:T(8,128)(2,1)}, u32[]{:S(2)}) copy-start(bf16[5,512,128]{1,2,0:T(8,128)(2,1)} %custom-call.2) | copy-start | bytes 1966084
  193.0 76.9 %collective-permute-start.6 = (bf16[512,640]{0,1:T(8,128)(2,1)S(1)}, bf16[512,640]{0,1:T(8,128)(2,1)S(1)}, u32[]{:S(2)}, u32[]{:S(2)}) collective-permute-start(bf16[512,640]{0,1:T(8,128)(2,1)S(1)} %copy.14), channel_id=1, source_target_pairs={{200,0},{208,8},{216,16},{224,24},{232,32},{240,40},{248,48},{0,56... | collective-permute-start | bytes 1966088 | tf_op jit(solution)/shard_map/ppermute | solution.py:13
  270.0 2.3 copy-start.2
  320.1 42.9 %copy-start.5 = (bf16[64,5120]{1,0:T(8,128)(2,1)S(1)}, bf16[64,5120]{1,0:T(8,128)(2,1)}, u32[]{:S(2)}) copy-start(bf16[64,5120]{1,0:T(8,128)(2,1)} %param.12) | copy-start | bytes 1966084
  320.1 42.9 %copy-start.6 = (bf16[64,5120]{1,0:T(8,128)(2,1)S(1)}, bf16[64,5120]{1,0:T(8,128)(2,1)}, u32[]{:S(2)}) copy-start(bf16[64,5120]{1,0:T(8,128)(2,1)} %param.21) | copy-start | bytes 1966084
  320.1 197.8 %all-reduce.2.cloned.1.call-start = ((), (), s32[]{:S(2)}) async-start(), calls=%async_computation.2 | async-start | bytes 1310720 | tf_op jit(solution)/shard_map/psum | solution.py:18
Sparse Core Ops, SparseCore 0:
  320.2 42.7 reduce-scatter.1
  366.4 151.4 all-reduce.1
where the time goes:
time: 527 us; the launch traced here: 526 us
  waiting for transfers between devices  397 us (75%)
  starting transfers between devices  40.5 us (8%)
  matrix products  37.9 us (7%)
  local copies, waits for them, and re-layouts  22.7 us (4%)
  between operations  15.6 us (3%)
  other arithmetic  12.3 us (2%)
    ppermute x14, waiting for transfers between devices, from_behind(): return lax.ppermute(block, axis, route)  203 us
    psum x1, waiting for transfers between devices, from_root(): return lax.psum(kept, axis)  152 us
    reduce_scatter x1, waiting for transfers between devices, body(): lax.psum_scatter(jnp.dot(attended, out_weight, preferred_element_type=jnp...  42.1 us
    ppermute x14, starting transfers between devices, from_behind(): return lax.ppermute(block, axis, route)  40.5 us
    unnamed x33, local copies, waits for them, and re-layouts  18.4 us
    dot_general x5, matrix products, one_head(): jnp.einsum('lqk,lkd->qd', weights.astype(jnp.bfloat16), value_blocks, pre...  16.1 us
    dot_general x5, matrix products, one_head(): jnp.einsum('qd,lkd->lqk', query, key_blocks, preferred_element_type=jnp.f...  12.8 us
  transfers between devices with their start and end apart: 16, of which 11 were waited for; matrix products, arithmetic and copies ran while one was open for 3% of the time, Pallas kernels for 0%

commit v1 on v0

v1 whole, which is shorter than its diff:
```python
import functools

import jax
import jax.numpy as jnp
from jax import lax
from jax.experimental import pallas as pl
from jax.experimental.pallas import tpu as pltpu
from jax.sharding import PartitionSpec as P

MESH = pl.DeviceIdType.MESH
HD = 128
ROWS = 512
WIDTH = 640
D = 5120
NY, NZ, NX = 4, 8, 4
SLOTS = NY * NZ
LAGS = 7
CHUNKS = 2
CROWS = 64 // CHUNKS
M = NX * CROWS
ITEMS = 10
N_ITEMS = CHUNKS * ITEMS
FAR = -1e30
SCALE2 = HD ** -0.5 * 1.4426950408889634
COLS = 1024
PARTS = D // COLS
NT = (((1,), (1,)), ((), ()))
ORDER = (0, 1, 7, 2, 6, 3, 5, 4)


def lanes(col, width):
    return jnp.concatenate([col] * (width // HD), axis=1)


def fold_max(x):
    return jnp.maximum(
        jnp.maximum(x[:, :128], x[:, 128:256]), jnp.maximum(x[:, 256:384], x[:, 384:])
    )


def fold_sum(x):
    return (x[:, :128] + x[:, 128:256]) + (x[:, 256:384] + x[:, 384:])


def kernel(
    latent_ref, q_ref, k_ref, v_ref, w_ref, gate_ref, levels_ref, offset_ref, mask_ref,
    fresh_ref, out_ref, rel_ref,
    wb, kv, qd, bias_all, os, a1, qv, kvv, vvv, o0, a0, s0, r0, s1, r1, u0, ry, u1, rz,
    lat, fre, gate_row, bias_own, sca, scb, ma, mb,
    load_sem, kv_ss, kv_rs, rel_ss, rel_rs, q_ss, q_rs, b_ss, b_rs, w_ss, w_rs,
    ft_ss, ft_rs, fy_ss, fy_rs, fty_ss, fty_rs, o0_sem, x0_ss, x0_rs, o_ss, o_rs,
    x1_ss, x1_rs, y_ss, y_rs, z_ss, z_rs,
):
    me = lax.axis_index("span")
    t = lax.axis_index("tp")
    y, z = me // NZ, me % NZ
    x, c = t // 2, t % 2
    twin_c = 1 - c

    def at(yy, zz, xx, cc):
        return (lax.rem(yy + NY, NY) * NZ + lax.rem(zz + NZ, NZ), lax.rem(xx + NX, NX) * 2 + cc)

    def slot_dev(shift):
        return (lax.rem(me + shift + SLOTS, SLOTS), t)

    twin = at(y, z, x, twin_c)

    def remote(src, dst, ss, rs, dev):
        return pltpu.make_async_remote_copy(
            src_ref=src, dst_ref=dst, send_sem=ss, recv_sem=rs, device_id=dev,
            device_id_type=MESH,
        )

    loads = [
        pltpu.make_async_copy(q_ref, qv, load_sem.at[0]),
        pltpu.make_async_copy(k_ref, kvv, load_sem.at[1]),
        pltpu.make_async_copy(v_ref, vvv, load_sem.at[2]),
        pltpu.make_async_copy(k_ref.at[:, pl.ds(512, 128)], kv.at[23, 0], load_sem.at[3]),
        pltpu.make_async_copy(v_ref.at[:, pl.ds(512, 128)], kv.at[23, 1], load_sem.at[4]),
        pltpu.make_async_copy(
            w_ref, wb.at[pl.ds(pl.multiple_of(c * WIDTH, 128), WIDTH)], load_sem.at[5]
        ),
        pltpu.make_async_copy(latent_ref, lat, load_sem.at[6]),
        pltpu.make_async_copy(fresh_ref, fre, load_sem.at[7]),
    ]
    for copy in loads:
        copy.start()
    q_loads = []
    for k in range(CHUNKS):
        for p in range(2):
            q_loads.append(
                pltpu.make_async_copy(
                    q_ref.at[:, p, pl.ds(CROWS * k, CROWS), pl.ds(512, 128)],
                    qd.at[k, 8 + p], load_sem.at[8 + 2 * k + p],
                )
            )
            q_loads[-1].start()

    barrier = pltpu.get_barrier_semaphore()
    partners = [twin]
    for dz in range(1, NZ):
        partners += [at(y, z + dz, x, c), at(y, z + dz, x, twin_c)]
    for dy in range(1, NY):
        partners.append(at(y + dy, z, x, c))
    for dx in range(1, NX):
        partners.append(at(y, z, x + dx, c))
    for shift in (1, -1, 7, -7):
        partners.append(slot_dev(shift))
    for dev in partners:
        pl.semaphore_signal(barrier, inc=1, device_id=dev, device_id_type=MESH)
    pl.semaphore_wait(barrier, len(partners))

    position = lax.rem(me - offset_ref[0] + SLOTS, SLOTS)
    lag_at = lax.broadcasted_iota(jnp.int32, (8, 128), 0)
    bias = jnp.zeros((8, 128), jnp.float32)
    for lag in range(1, LAGS + 1):
        ok = (mask_ref[0, lag - 1] == 1) & (position >= lag)
        bias = jnp.where(lag_at == lag, jnp.where(ok, 0.0, FAR), bias)
    bias_own[...] = bias
    bias_all[8] = bias
    bias_all[9] = bias
    level = levels_ref[0]
    row = gate_ref[0:1, :]
    for i in range(1, 4):
        row = jnp.where(level == i, gate_ref[i : i + 1, :], row)
    gate_row[...] = row * 0.25

    def kv_send(j, hf, which):
        ref = (k_ref, v_ref)[which]
        src = ref.at[pl.ds(256 * hf, 256), pl.ds(128 * j, 128)]
        dst = kv.at[8 + z, which, pl.ds(256 * hf, 256)]
        d = 4 * c + j
        return src, dst, kv_ss.at[j, hf, which], kv_rs.at[z, which], d, hf

    def q_send(j, hf, k):
        src = q_ref.at[:, hf, pl.ds(CROWS * k, CROWS), pl.ds(128 * j, 128)]
        dst = qd.at[k, z]
        return src, dst, q_ss.at[j, hf, k], q_rs.at[k, z], 4 * c + j, hf

    def b_send(j, hf):
        return bias_own, bias_all.at[z], b_ss.at[j, hf], b_rs.at[z], 4 * c + j, hf

    def go(args):
        src, dst, ss, rs, d, hf = args
        mine = (d == z) & (c == hf)

        @pl.when(mine)
        def _():
            pltpu.make_async_copy(src, dst, rs).start()

        @pl.when(jnp.logical_not(mine))
        def _():
            remote(src, dst, ss, rs, at(y, d, x, hf)).start()

    def gone(args):
        src, dst, ss, rs, d, hf = args

        @pl.when(jnp.logical_not((d == z) & (c == hf)))
        def _():
            remote(src, dst, ss, rs, at(y, d, x, hf)).wait_send()

    def lag_slot(lag):
        return 16 + 7 - lag

    def relay_first(which, ahead):
        ref = (k_ref, v_ref)[which]
        return remote(
            ref.at[:, pl.ds(512, 128)], kv.at[lag_slot(7 if ahead else 1), which],
            rel_ss.at[ahead, which], rel_rs.at[ahead, which],
            slot_dev(7 if ahead else 1),
        )

    def relay_next(step, ahead):
        old, new = (8 - step, 7 - step) if ahead else (step, step + 1)
        part = pl.ds(0, 512) if step < 3 else pl.ds(256 * ahead, 256)
        return remote(
            kv.at[lag_slot(old), :, part], kv.at[lag_slot(new), :, part],
            rel_ss.at[ahead, 1 + step], rel_rs.at[ahead, 1 + step],
            slot_dev(-1 if ahead else 1),
        )

    for which in range(2):
        for j in range(4):
            for hf in range(2):
                go(kv_send(j, hf, which))
    for ahead in range(2):
        for which in range(2):
            relay_first(which, ahead).start()
    for j in range(4):
        for hf in range(2):
            go(b_send(j, hf))
    w_send = remote(
        w_ref, wb.at[pl.ds(pl.multiple_of(c * WIDTH, 128), WIDTH)], w_ss.at[0], w_rs.at[0], twin
    )
    w_send.start()
    for k in range(CHUNKS):
        for j in range(4):
            for hf in range(2):
                go(q_send(j, hf, k))

    for copy in loads[:3]:
        copy.wait()

    def head_at_home(i, carry):
        head, half = i // 2, i % 2
        col = pl.ds(pl.multiple_of(head * 128, 128), 128)
        q = qv[pl.ds(2 * half, 2), :, :, col].reshape(256, HD)
        s = lax.dot_general(q, kvv[:, col], NT, preferred_element_type=jnp.float32)
        top = jnp.max(fold_max(s), axis=1, keepdims=True) * SCALE2
        p = jnp.exp2(s * SCALE2 - top)
        total = jnp.sum(fold_sum(p), axis=1, keepdims=True)
        o = jnp.dot(p.astype(jnp.bfloat16), vvv[:, col], preferred_element_type=jnp.float32)
        o0[pl.ds(2 * half, 2), :, :, col] = (
            (o / total).astype(jnp.bfloat16).reshape(2, 2, 64, HD)
        )
        return carry

    lax.fori_loop(0, 10, head_at_home, 0)
    own_cols = pl.ds(pl.multiple_of(c * WIDTH, 128), WIDTH)
    o0_own = pltpu.make_async_copy(o0.at[:, c], a0.at[:, :, own_cols], o0_sem.at[0])
    o0_twin = remote(
        o0.at[:, twin_c], a0.at[:, :, own_cols], o0_sem.at[1], o0_sem.at[2], twin
    )
    o0_own.start()
    o0_twin.start()

    half = pl.ds(pl.multiple_of(256 * c, 256), 256)
    other = pl.ds(pl.multiple_of(256 * twin_c, 256), 256)

    def to_twin(src_z):
        ref = kv.at[8 + src_z, :, half]
        return remote(ref, ref, ft_ss.at[src_z], ft_rs.at[src_z], twin)

    def to_next(src_z):
        return remote(
            kv.at[8 + src_z, :, half], kv.at[src_z, :, half], fy_ss.at[src_z],
            fy_rs.at[src_z], at(y + 1, z, x, c),
        )

    def prev_to_twin(src_z):
        ref = kv.at[src_z, :, half]
        return remote(ref, ref, fty_ss.at[src_z], fty_rs.at[src_z], twin)

    def pass_on(shift):
        src_z = lax.rem(z + shift, NZ)
        for which in range(2):
            ref = kv.at[8 + src_z, which, half]
            pltpu.make_async_copy(ref, ref, kv_rs.at[src_z, which]).wait()
        to_next(src_z).start()
        to_twin(src_z).start()

    def pass_prev(shift):
        src_z = lax.rem(z + shift, NZ)
        to_next(src_z).wait_recv()
        prev_to_twin(src_z).start()

    def project(a_ref, s_ref, r_ref, rows, ss, rs):
        def part(n, carry):
            for h in range(2):
                col = pl.ds(pl.multiple_of(n * COLS + h * 512, 512), 512)
                a = a_ref[...].reshape(NX * rows, 2 * WIDTH)
                out = jnp.dot(a, wb[:, col], preferred_element_type=jnp.float32)
                s_ref[:, :, col] = out.astype(jnp.bfloat16).reshape(NX, rows, 512)
            for dx in range(1, NX):
                x_send(s_ref, r_ref, ss, rs, n, dx).start()
            return carry

        lax.fori_loop(0, PARTS, part, 0)

    def x_send(s_ref, r_ref, ss, rs, n, dx):
        col = pl.ds(pl.multiple_of(n * COLS, COLS), COLS)
        to_x = lax.rem(x + dx, NX)
        return remote(
            s_ref.at[to_x, :, col], r_ref.at[3 - dx, :, col], ss.at[n, dx - 1],
            rs.at[n, 3 - dx], at(y, z, to_x, c),
        )

    def gather_x(s_ref, r_ref, ss, rs, n, lat_rows, write):
        for dx in range(1, NX):
            x_send(s_ref, r_ref, ss, rs, n, dx).wait_recv()
        for h in range(2):
            col = pl.ds(pl.multiple_of(n * COLS + h * 512, 512), 512)
            total = s_ref[x, :, col].astype(jnp.float32)
            for i in range(3):
                total = total + r_ref[i, :, col].astype(jnp.float32)
            updated = lat[lat_rows, col].astype(jnp.float32) - gate_row[:, col] * total
            write(col, updated.astype(jnp.bfloat16))

    def sent_x(s_ref, r_ref, ss, rs):
        def part(n, carry):
            for dx in range(1, NX):
                x_send(s_ref, r_ref, ss, rs, n, dx).wait_send()
            return carry

        lax.fori_loop(0, PARTS, part, 0)

    pass_on(0)
    pass_on(1)
    pass_on(7)
    for ahead in range(2):
        for which in range(2):
            relay_first(which, ahead).wait_recv()
        relay_next(1, ahead).start()

    for copy in loads[5:]:
        copy.wait()
    w_send.wait_recv()
    o0_own.wait()
    o0_twin.wait_recv()
    project(a0, s0, r0, 64, x0_ss, x0_rs)

    pass_on(2)
    pass_on(6)
    for shift in (0, 1, 7):
        pass_prev(shift)
    for ahead in range(2):
        relay_next(1, ahead).wait_recv()
        relay_next(2, ahead).start()
    pass_on(3)
    pass_on(5)
    pass_on(4)

    oldest = position == 0

    def write_u0(col, updated):
        u0[:, col] = jnp.where(oldest, updated, jnp.zeros_like(updated))

    def finish0(n, carry):
        gather_x(s0, r0, x0_ss, x0_rs, n, slice(None), write_u0)
        return carry

    for ahead in range(2):
        relay_next(2, ahead).wait_recv()
        relay_next(3, ahead).start()
    for shift in (2, 6, 3, 5, 4):
        pass_prev(shift)

    lax.fori_loop(0, PARTS, finish0, 0)
    y_width = D // NY

    def y_send(dy):
        to_y = lax.rem(y + dy, NY)
        return remote(
            u0.at[:, pl.ds(pl.multiple_of(to_y * y_width, 128), y_width)], ry.at[3 - dy],
            y_ss.at[dy - 1], y_rs.at[3 - dy], at(to_y, z, x, c),
        )

    for dy in range(1, NY):
        y_send(dy).start()

    def z_window(zz):
        return pl.ds(pl.multiple_of((zz * 160 // 128) * 128, 128), 256)

    def z_send(dz):
        to_z = lax.rem(z + dz, NZ)
        return remote(
            u1.at[:, z_window(to_z)], rz.at[7 - dz], z_ss.at[dz - 1], z_rs.at[7 - dz],
            at(y, to_z, x, c),
        )

    def share_y():
        for dy in range(1, NY):
            y_send(dy).wait_recv()
        total = u0[:, pl.ds(pl.multiple_of(y * y_width, 128), y_width)].astype(jnp.float32)
        for i in range(3):
            total = total + ry[i].astype(jnp.float32)
        u1[...] = total.astype(jnp.bfloat16)
        for dz in range(1, NZ):
            z_send(dz).start()

    def share_z():
        for dz in range(1, NZ):
            z_send(dz).wait_recv()
        total = u1[:, z_window(z)].astype(jnp.float32)
        for i in range(7):
            total = total + rz[i].astype(jnp.float32)
        turned = pltpu.roll(total, lax.rem(256 - (z % 4) * 32, 256), 1)
        rel_ref[...] = turned[:, :160].astype(jnp.bfloat16)

    for copy in loads[3:5] + q_loads:
        copy.wait()
    for ahead in range(2):
        relay_next(3, ahead).wait_recv()
    for src_z in range(NZ):
        to_twin(src_z).wait_recv()
        prev_to_twin(src_z).wait_recv()

    def item(it):
        k, j = it // ITEMS, it % ITEMS
        off = jnp.where(j % 2 == 1, (j + 1) // 2, NZ - j // 2)
        s = jnp.where(j < 8, lax.rem(z + off, NZ), j)
        return k, j, s, jnp.where(j < 8, s + 1, 16)

    def o_send(it):
        k, j, s, _ = item(it)
        gathered = j < 8
        to_z = jnp.where(gathered, s, z)
        to_c = jnp.where(gathered, c, j - 8)
        head_col = jnp.where(gathered, (z // 4) * WIDTH + (z % 4) * HD, c * WIDTH + 4 * HD)
        dst = a1.at[k, :, :, pl.ds(pl.multiple_of(head_col, 128), 128)]
        rs = o_rs.at[k, jnp.where(gathered, z, 8 + c)]
        return os.at[k, s], dst, o_ss.at[k, s], rs, to_z, to_c

    def arrived(it):
        k, j, s, _ = item(it)

        @pl.when(j < 8)
        def _():
            pltpu.make_async_copy(qd.at[k, s], qd.at[k, s], q_rs.at[k, s]).wait()

        @pl.when((j < 8) & (k == 0))
        def _():
            pltpu.make_async_copy(bias_all.at[s], bias_all.at[s], b_rs.at[s]).wait()

    def first_pass(q, s, base, i, sc, top):
        scores = lax.dot_general(q, kv[base + i, 0], NT, preferred_element_type=jnp.float32)
        sc[i] = scores
        return jnp.maximum(top, fold_max(scores) * SCALE2 + bias_all[s, 7 - i : 8 - i, :])

    def second_pass(s, base, i, sc, top, total, acc):
        p = jnp.exp2(sc[i] * SCALE2 - lanes(top - bias_all[s, 7 - i : 8 - i, :], 512))
        acc = acc + jnp.dot(
            p.astype(jnp.bfloat16), kv[base + i, 1], preferred_element_type=jnp.float32
        )
        return total + fold_sum(p), acc

    def row_top(top):
        return jnp.broadcast_to(jnp.max(top, axis=1, keepdims=True), (M, HD))

    def stage(it, sc, m_ref, next_sc, next_m, last=False):
        k, j, s, base = item(it)
        if not last:
            arrived(it + 1)
            k2, _, s2, base2 = item(it + 1)
            q = qd[k2, s2].reshape(M, HD)
        top = m_ref[...]
        next_top = jnp.full((M, HD), FAR, jnp.float32)
        total = jnp.zeros((M, HD), jnp.float32)
        acc = jnp.zeros((M, HD), jnp.float32)
        for i in range(8):
            if not last:
                next_top = first_pass(q, s2, base2, i, next_sc, next_top)
            total, acc = second_pass(s, base, i, sc, top, total, acc)
        if not last:
            next_m[...] = row_top(next_top)
        o = acc / jnp.sum(total, axis=1, keepdims=True)
        os[k, s] = o.astype(jnp.bfloat16).reshape(NX, CROWS, HD)
        src, dst, ss, rs, to_z, to_c = o_send(it)
        mine = (to_z == z) & (to_c == c)

        @pl.when(mine)
        def _():
            pltpu.make_async_copy(src, dst, rs).start()

        @pl.when(jnp.logical_not(mine))
        def _():
            remote(src, dst, ss, rs, at(y, to_z, x, to_c)).start()

    def project_chunk(k):
        for h in range(10):
            ref = a1.at[k, :, :, pl.ds(0, 128)]
            pltpu.make_async_copy(ref, ref, o_rs.at[k, h]).wait()
        project(a1.at[k], s1.at[k], r1.at[k], CROWS, x1_ss.at[k], x1_rs.at[k])

    arrived(0)
    k, _, s, base = item(0)
    q = qd[k, s].reshape(M, HD)
    top = jnp.full((M, HD), FAR, jnp.float32)
    for i in range(8):
        top = first_pass(q, s, base, i, sca, top)
    ma[...] = row_top(top)

    def pair(j, carry):
        stage(2 * j, sca, ma, scb, mb)

        @pl.when(j < N_ITEMS // 2 - 1)
        def _():
            stage(2 * j + 1, scb, mb, sca, ma)

        @pl.when(j == 1)
        def _():
            share_y()

        @pl.when(j == 3)
        def _():
            share_z()

        @pl.when(j == 6)
        def _():
            project_chunk(0)

        return carry

    lax.fori_loop(0, N_ITEMS // 2, pair, 0)
    stage(N_ITEMS - 1, scb, mb, sca, ma, last=True)
    project_chunk(1)

    def finish(k):
        rows = pl.ds(CROWS * k, CROWS)

        def write(col, updated):
            out_ref[rows, col] = jnp.where(oldest, fre[rows, col], updated)

        def part(n, carry):
            gather_x(s1.at[k], r1.at[k], x1_ss.at[k], x1_rs.at[k], n, rows, write)
            return carry

        lax.fori_loop(0, PARTS, part, 0)

    finish(0)
    finish(1)

    for which in range(2):
        for j in range(4):
            for hf in range(2):
                gone(kv_send(j, hf, which))
    for ahead in range(2):
        for which in range(2):
            relay_first(which, ahead).wait_send()
        for step in range(1, 4):
            relay_next(step, ahead).wait_send()
    for j in range(4):
        for hf in range(2):
            gone(b_send(j, hf))
            for k in range(CHUNKS):
                gone(q_send(j, hf, k))
    w_send.wait_send()
    o0_twin.wait_send()
    for src_z in range(NZ):
        to_twin(src_z).wait_send()
        to_next(src_z).wait_send()
        prev_to_twin(src_z).wait_send()
    sent_x(s0, r0, x0_ss, x0_rs)
    for k in range(CHUNKS):
        sent_x(s1.at[k], r1.at[k], x1_ss.at[k], x1_rs.at[k])
    for dy in range(1, NY):
        y_send(dy).wait_send()
    for dz in range(1, NZ):
        z_send(dz).wait_send()

    def o_gone(it, carry):
        src, dst, ss, rs, to_z, to_c = o_send(it)

        @pl.when(jnp.logical_not((to_z == z) & (to_c == c)))
        def _():
            remote(src, dst, ss, rs, at(y, to_z, x, to_c)).wait_send()

        return carry

    lax.fori_loop(0, N_ITEMS, o_gone, 0)


def body(
    latent, queries, keys, values, out_weight, level_gate, levels, offset, lag_mask, fresh_noise
):
    bf16, f32 = jnp.bfloat16, jnp.float32
    hbm = pl.BlockSpec(memory_space=pl.ANY)
    vmem = pl.BlockSpec(memory_space=pltpu.VMEM)
    smem = pl.BlockSpec(memory_space=pltpu.SMEM)
    dma = pltpu.SemaphoreType.DMA
    vm = pltpu.VMEM
    scratch = [
        vm((2 * WIDTH, D), bf16),
        vm((24, 2, ROWS, HD), bf16),
        vm((CHUNKS, ITEMS, NX, CROWS, HD), bf16),
        vm((ITEMS, 8, 128), f32),
        vm((CHUNKS, ITEMS, NX, CROWS, HD), bf16),
        vm((CHUNKS, NX, CROWS, 2 * WIDTH), bf16),
        vm((NX, 2, 64, WIDTH), bf16),
        vm((ROWS, WIDTH), bf16),
        vm((ROWS, WIDTH), bf16),
        vm((NX, 2, 64, WIDTH), bf16),
        vm((NX, 64, 2 * WIDTH), bf16),
        vm((NX, 64, D), bf16),
        vm((NX - 1, 64, D), bf16),
        vm((CHUNKS, NX, CROWS, D), bf16),
        vm((CHUNKS, NX - 1, CROWS, D), bf16),
        vm((64, D), bf16),
        vm((NY - 1, 64, D // NY), bf16),
        vm((64, D // NY), bf16),
        vm((NZ - 1, 64, 256), bf16),
        vm((64, D), bf16),
        vm((64, D), bf16),
        vm((1, D), f32),
        vm((8, 128), f32),
        vm((8, M, ROWS), f32),
        vm((8, M, ROWS), f32),
        vm((M, HD), f32),
        vm((M, HD), f32),
        dma((8 + 2 * CHUNKS,)),
        dma((4, 2, 2)), dma((NZ, 2)),
        dma((2, 5)), dma((2, 5)),
        dma((4, 2, CHUNKS)), dma((CHUNKS, NZ)),
        dma((4, 2)), dma((NZ,)),
        dma((1,)), dma((1,)),
        dma((NZ,)), dma((NZ,)),
        dma((NZ,)), dma((NZ,)),
        dma((NZ,)), dma((NZ,)),
        dma((3,)),
        dma((PARTS, 3)), dma((PARTS, 3)),
        dma((CHUNKS, ITEMS)), dma((CHUNKS, ITEMS)),
        dma((CHUNKS, PARTS, 3)), dma((CHUNKS, PARTS, 3)),
        dma((3,)), dma((3,)),
        dma((7,)), dma((7,)),
    ]
    return pl.pallas_call(
        kernel,
        out_shape=(
            jax.ShapeDtypeStruct((64, D), bf16),
            jax.ShapeDtypeStruct((64, 160), bf16),
        ),
        in_specs=[hbm, hbm, hbm, hbm, hbm, vmem, smem, smem, smem, hbm],
        out_specs=(vmem, vmem),
        scratch_shapes=scratch,
        compiler_params=pltpu.CompilerParams(
            collective_id=1, has_side_effects=True, vmem_limit_bytes=56 << 20
        ),
        name="window_step",
    )(
        latent, queries.reshape(NX, 2, 64, WIDTH), keys, values, out_weight, level_gate,
        levels, offset, lag_mask, fresh_noise,
    )


def solution(mesh):
    return jax.shard_map(
        body,
        mesh=mesh,
        in_specs=(
            P(("span", "tp"), None),
            P("span", "tp"),
            P("span", "tp"),
            P("span", "tp"),
            P("tp", None),
            P(),
            P("span"),
            P(),
            P("span", None),
            P("tp", None),
        ),
        out_specs=(P(("span", "tp"), None), P("tp", "span")),
        check_vma=False,
    )
```

time: 527 us -> 143 us (0.27)
  waiting for transfers between devices: 397 us -> 0 us
  Pallas kernels: 0 us -> 135 us
  starting transfers between devices: 40.5 us -> 0 us
  matrix products: 37.9 us -> 0 us
  local copies, waits for them, and re-layouts: 22.7 us -> 3.34 us
  between operations: 15.6 us -> 1.93 us
  other arithmetic: 12.3 us -> 0 us
    ppermute x14 -> x0, waiting for transfers between devices: 203 us -> none  [from_behind(): return lax.ppermute(block, axis, route)]
    psum x1 -> x0, waiting for transfers between devices: 152 us -> none  [from_root(): return lax.psum(kept, axis)]
    pallas_call x0 -> x1, Pallas kernels: none -> 135 us  [body(): pl.pallas_call(kernel, out_shape=(jax.ShapeDtypeStruct((64, D), bf16), ja...]
    reduce_scatter x1 -> x0, waiting for transfers between devices: 42.1 us -> none  [body(): lax.psum_scatter(jnp.dot(attended, out_weight, preferred_element_type=jnp...]
    ppermute x14 -> x0, starting transfers between devices: 40.5 us -> none  [from_behind(): return lax.ppermute(block, axis, route)]
    dot_general x11 -> x0, matrix products: 37.9 us -> none  [the longest x5 16.1 us: one_head(): jnp.einsum('lqk,lkd->qd', weights.astype(jnp.bfloat16), value_blocks, pre...]
    unnamed x33 -> x2, local copies, waits for them, and re-layouts: 18.4 us -> 3.34 us
    reduce_sum x5 -> x0, other arithmetic: 9.01 us -> none  [one_head(): row_total = jnp.sum(weights, axis=(0, 2))]
  transfers between devices with their start and end apart: 16 -> 0, of which waited for: 11 -> 0; matrix products, arithmetic and copies ran while one was open for 3% -> 0% of each run, Pallas kernels for 0% -> 0%
where the time goes in v1:
time: 143 us; the launch traced here: 140 us
  Pallas kernels  135 us (94%)
  local copies, waits for them, and re-layouts  3.34 us (2%)
  between operations  1.93 us (1%)
    pallas_call x1, Pallas kernels, body(): pl.pallas_call(kernel, out_shape=(jax.ShapeDtypeStruct((64, D), bf16), ja...  135 us
    unnamed x2, local copies, waits for them, and re-layouts  3.34 us

profile of v1, /device:TPU:2, one launch (start us, length us, event | category | flops | bytes accessed | tf_op | source)
XLA Modules:
  0.0 140.2 jit_solution(15594687195073823285)
XLA Ops:
  1.9 135.0 %window_step.1 = (bf16[64,5120]{1,0:T(8,128)(2,1)}, bf16[64,160]{1,0:T(8,128)(2,1)}) custom-call(bf16[64,5120]{1,0:T(8,128)(2,1)} %latent_ref.1, bf16[4,2,64,640]{3,2,1,0:T(8,128)(2,1)} %bitcast.1, bf16[512,640]{1,0:T(8,128)(2,1)} %k_ref.1, bf16[512,640]{1,0:T(8,128)(2,1)} %v_ref.1, bf16[640,5120]{1,0:T(8,128)(2,1)} %w_ref.1, f32[4,5120]{1,0:T(4,128)} %gate_ref.1, ...), custom_call_target="tpu_custom_call" | custom-call | tf_op jit(solution)/shard_map/window_step/pallas_call | solution.py:606
  136.9 2.0 %copy.16 = bf16[64,5120]{1,0:T(8,128)(2,1)} copy(bf16[64,5120]{1,0:T(8,128)(2,1)} %get-tuple-element.4) | data formatting | bytes 1310720
  138.9 1.4 copy.17

commit v2 on v1

v2 whole, which is shorter than its diff:
```python
import functools

import jax
import jax.numpy as jnp
from jax import lax
from jax.experimental import pallas as pl
from jax.experimental.pallas import tpu as pltpu
from jax.sharding import PartitionSpec as P

MESH = pl.DeviceIdType.MESH
HD = 128
ROWS = 512
WIDTH = 640
D = 5120
NY, NZ, NX = 4, 8, 4
SLOTS = NY * NZ
LAGS = 7
CHUNKS = 2
CROWS = 64 // CHUNKS
M = NX * CROWS
ITEMS = 10
N_ITEMS = CHUNKS * ITEMS
FAR = -1e30
SCALE2 = HD ** -0.5 * 1.4426950408889634
COLS = 1024
PARTS = D // COLS
NT = (((1,), (1,)), ((), ()))
FIRST_STAY = 12
PLAN = {1: ("r3",), 5: ("fr",), 7: ("p0",)}


def lanes(col, width):
    return jnp.concatenate([col] * (width // HD), axis=1)


def fold_max(x):
    return jnp.maximum(
        jnp.maximum(x[:, :128], x[:, 128:256]), jnp.maximum(x[:, 256:384], x[:, 384:])
    )


def fold_sum(x):
    return (x[:, :128] + x[:, 128:256]) + (x[:, 256:384] + x[:, 384:])


def kernel(
    latent_ref, q_ref, k_ref, v_ref, w_ref, gate_ref, levels_ref, offset_ref, mask_ref,
    fresh_ref, out_ref, rel_ref,
    wb, kv, qd, bias_all, os, a1, qv, kvv, vvv, o0, a0, s0, r0, s1, r1, u0, ry, u1, rz,
    new, lat, fre, gate_row, bias_own, sca, scb, ma, mb,
    load_sem, kv_ss, kv_rs, rel_ss, rel_rs, q_ss, q_rs, b_ss, b_rs, w_ss, w_rs,
    ft_ss, ft_rs, fy_ss, fy_rs, fty_ss, fty_rs, o0_sem, x0_ss, x0_rs, o_ss, o_rs,
    x1_ss, x1_rs, out_sem, y_ss, y_rs, z_ss, z_rs,
):
    me = lax.axis_index("span")
    t = lax.axis_index("tp")
    y, z = me // NZ, me % NZ
    x, c = t // 2, t % 2
    twin_c = 1 - c

    def at(yy, zz, xx, cc):
        return (lax.rem(yy + NY, NY) * NZ + lax.rem(zz + NZ, NZ), lax.rem(xx + NX, NX) * 2 + cc)

    def slot_dev(shift):
        return (lax.rem(me + shift + SLOTS, SLOTS), t)

    twin = at(y, z, x, twin_c)

    def remote(src, dst, ss, rs, dev):
        return pltpu.make_async_remote_copy(
            src_ref=src, dst_ref=dst, send_sem=ss, recv_sem=rs, device_id=dev,
            device_id_type=MESH,
        )

    def settle(ref, sem):
        pltpu.make_async_copy(ref, ref, sem).wait()

    loads = [
        pltpu.make_async_copy(q_ref, qv, load_sem.at[0]),
        pltpu.make_async_copy(k_ref, kvv, load_sem.at[1]),
        pltpu.make_async_copy(v_ref, vvv, load_sem.at[2]),
        pltpu.make_async_copy(k_ref.at[:, pl.ds(512, 128)], kv.at[23, 0], load_sem.at[3]),
        pltpu.make_async_copy(v_ref.at[:, pl.ds(512, 128)], kv.at[23, 1], load_sem.at[3]),
        pltpu.make_async_copy(
            w_ref, wb.at[pl.ds(pl.multiple_of(c * WIDTH, 128), WIDTH)], load_sem.at[5]
        ),
        pltpu.make_async_copy(latent_ref, lat, load_sem.at[6]),
        pltpu.make_async_copy(fresh_ref, fre, load_sem.at[7]),
    ]
    for copy in loads:
        copy.start()
    q_loads = []
    for k in range(CHUNKS):
        for p in range(2):
            q_loads.append(
                pltpu.make_async_copy(
                    q_ref.at[:, p, pl.ds(CROWS * k, CROWS), pl.ds(512, 128)],
                    qd.at[k, 8 + p], load_sem.at[4],
                )
            )
            q_loads[-1].start()

    barrier = pltpu.get_barrier_semaphore()
    partners = [twin]
    for dz in range(1, NZ):
        partners += [at(y, z + dz, x, c), at(y, z + dz, x, twin_c)]
    for dy in range(1, NY):
        partners.append(at(y + dy, z, x, c))
    for dx in range(1, NX):
        partners.append(at(y, z, x + dx, c))
    for shift in (1, -1, 7, -7):
        partners.append(slot_dev(shift))
    for dev in partners:
        pl.semaphore_signal(barrier, inc=1, device_id=dev, device_id_type=MESH)
    pl.semaphore_wait(barrier, len(partners))

    position = lax.rem(me - offset_ref[0] + SLOTS, SLOTS)
    lag_at = lax.broadcasted_iota(jnp.int32, (8, 128), 0)
    bias = jnp.zeros((8, 128), jnp.float32)
    for lag in range(1, LAGS + 1):
        ok = (mask_ref[0, lag - 1] == 1) & (position >= lag)
        bias = jnp.where(lag_at == lag, jnp.where(ok, 0.0, FAR), bias)
    bias_own[...] = bias
    bias_all[8] = bias
    bias_all[9] = bias
    level = levels_ref[0]
    row = gate_ref[0:1, :]
    for i in range(1, 4):
        row = jnp.where(level == i, gate_ref[i : i + 1, :], row)
    gate_row[...] = row * 0.25

    def turned(i):
        return lax.rem(z + i, 4)

    def head_cols(j):
        return pl.ds(pl.multiple_of(128 * j, 128), 128)

    def kv_send(i, hf, which):
        j = turned(i)
        ref = (k_ref, v_ref)[which]
        src = ref.at[pl.ds(256 * hf, 256), head_cols(j)]
        dst = kv.at[8 + z, which, pl.ds(256 * hf, 256)]
        d = 4 * c + j
        return src, dst, kv_ss.at[0], kv_rs.at[z], d, hf

    def q_send(i, hf, k):
        j = turned(i)
        src = q_ref.at[:, hf, pl.ds(CROWS * k, CROWS), head_cols(j)]
        dst = qd.at[k, z]
        return src, dst, q_ss.at[0], q_rs.at[k, z], 4 * c + j, hf

    def b_send(j, hf):
        return bias_own, bias_all.at[z], b_ss.at[0], b_rs.at[0], 4 * c + j, hf

    def go(args):
        src, dst, ss, rs, d, hf = args
        mine = (d == z) & (c == hf)

        @pl.when(mine)
        def _():
            pltpu.make_async_copy(src, dst, rs).start()

        @pl.when(jnp.logical_not(mine))
        def _():
            remote(src, dst, ss, rs, at(y, d, x, hf)).start()

    def lag_slot(lag):
        return 16 + 7 - lag

    def relay_first(which, ahead):
        ref = (k_ref, v_ref)[which]
        return remote(
            ref.at[:, pl.ds(512, 128)], kv.at[lag_slot(7 if ahead else 1), which],
            rel_ss.at[0], rel_rs.at[ahead, 0],
            slot_dev(7 if ahead else 1),
        )

    def relay_next(step, ahead):
        old, new = (8 - step, 7 - step) if ahead else (step, step + 1)
        part = pl.ds(0, 512) if step < 3 else pl.ds(256 * ahead, 256)
        return remote(
            kv.at[lag_slot(old), :, part], kv.at[lag_slot(new), :, part],
            rel_ss.at[0], rel_rs.at[ahead, step],
            slot_dev(-1 if ahead else 1),
        )

    def send_kv(steps_of):
        for i in steps_of:
            for hf in range(2):
                for which in range(2):
                    go(kv_send(i, hf, which))

    def send_q(k):
        for i in range(4):
            for hf in range(2):
                go(q_send(i, hf, k))

    for ahead in range(2):
        for which in range(2):
            relay_first(which, ahead).start()
    send_kv((0, 1))
    for j in range(4):
        for hf in range(2):
            go(b_send(j, hf))
    w_send = remote(
        w_ref, wb.at[pl.ds(pl.multiple_of(c * WIDTH, 128), WIDTH)], w_ss.at[0], w_rs.at[0], twin
    )
    w_send.start()

    for copy in loads[:3]:
        copy.wait()

    def head_at_home(i, carry):
        head, half = i // 2, i % 2
        col = pl.ds(pl.multiple_of(head * 128, 128), 128)
        q = qv[pl.ds(2 * half, 2), :, :, col].reshape(256, HD)
        s = lax.dot_general(q, kvv[:, col], NT, preferred_element_type=jnp.float32)
        top = jnp.max(fold_max(s), axis=1, keepdims=True) * SCALE2
        p = jnp.exp2(s * SCALE2 - top)
        total = jnp.sum(fold_sum(p), axis=1, keepdims=True)
        o = jnp.dot(p.astype(jnp.bfloat16), vvv[:, col], preferred_element_type=jnp.float32)
        o0[pl.ds(2 * half, 2), :, :, col] = (
            (o / total).astype(jnp.bfloat16).reshape(2, 2, 64, HD)
        )
        return carry

    lax.fori_loop(0, 10, head_at_home, 0)
    own_cols = pl.ds(pl.multiple_of(c * WIDTH, 128), WIDTH)
    o0_own = pltpu.make_async_copy(o0.at[:, c], a0.at[:, :, own_cols], o0_sem.at[0])
    o0_twin = remote(
        o0.at[:, twin_c], a0.at[:, :, own_cols], o0_sem.at[1], o0_sem.at[2], twin
    )
    o0_own.start()
    o0_twin.start()

    half = pl.ds(pl.multiple_of(256 * c, 256), 256)
    other = pl.ds(pl.multiple_of(256 * twin_c, 256), 256)

    def to_twin(src_z):
        ref = kv.at[8 + src_z, :, half]
        return remote(ref, ref, ft_ss.at[0], ft_rs.at[0], twin)

    def to_next(src_z):
        return remote(
            kv.at[8 + src_z, :, half], kv.at[src_z, :, half], fy_ss.at[0],
            fy_rs.at[src_z], at(y + 1, z, x, c),
        )

    def prev_to_twin(src_z):
        ref = kv.at[src_z, :, half]
        return remote(ref, ref, fty_ss.at[0], fty_rs.at[src_z], twin)

    def pass_on(i):
        for far in range(2):
            src_z = lax.rem(z - i + NZ, 4) + 4 * far
            settle(kv.at[8 + src_z, :, half], kv_rs.at[src_z])
            pl.when(src_z > 0)(lambda: to_next(src_z).start())
            to_twin(src_z).start()

    def pass_prev(src_z):
        to_next(src_z).wait_recv()
        prev_to_twin(src_z).start()

    def relay(step):
        for ahead in range(2):
            if step == 1:
                settle(kv.at[lag_slot(7 if ahead else 1)], rel_rs.at[ahead, 0])
            else:
                relay_next(step - 1, ahead).wait_recv()
            if step < 4:
                relay_next(step, ahead).start()

    def half_cols(n, h):
        return pl.ds(pl.multiple_of(n * COLS + h * 512, 512), 512)

    def part_cols(n):
        return pl.ds(pl.multiple_of(n * COLS, COLS), COLS)

    right, left = lax.rem(x + 1, NX), lax.rem(x + 3, NX)
    opposite = lax.rem(x + 2, NX)

    def x_via(bufs, n, h):
        s_ref, r_ref, ss, rs = bufs
        ref = half_cols(n, h)
        return remote(
            s_ref.at[opposite, :, ref], r_ref.at[2, :, ref], ss, rs.at[n, 0],
            at(y, z, left if h else right, c),
        )

    def x_last(bufs, n, h):
        s_ref, r_ref, ss, rs = bufs
        to_x = left if h else right
        return remote(
            s_ref.at[to_x, :, part_cols(n)], r_ref.at[h, :, part_cols(n)], ss,
            rs.at[n, 1], at(y, z, to_x, c),
        )

    def add_on(bufs):
        lax.fori_loop(0, PARTS, functools.partial(add_part, bufs), 0)

    def add_part(bufs, n, carry):
        s_ref, r_ref, _, rs = bufs
        settle(r_ref.at[2, :, part_cols(n)], rs.at[n, 0])
        for h in range(2):
            to_x = left if h else right
            ref = half_cols(n, h)
            total = s_ref[to_x, :, ref].astype(jnp.float32) + r_ref[2, :, ref].astype(jnp.float32)
            s_ref[to_x, :, ref] = total.astype(jnp.bfloat16)
            x_last(bufs, n, h).start()
        return carry

    def project(a_ref, bufs, rows):
        s_ref = bufs[0]

        def part(n, carry):
            for h in range(2):
                col = half_cols(n, h)
                a = a_ref[...].reshape(NX * rows, 2 * WIDTH)
                out = jnp.dot(a, wb[:, col], preferred_element_type=jnp.float32)
                s_ref[:, :, col] = out.astype(jnp.bfloat16).reshape(NX, rows, 512)
                x_via(bufs, n, h).start()
            return carry

        lax.fori_loop(0, PARTS, part, 0)

    def gather_x(bufs, n, lat_rows, write):
        s_ref, r_ref, _, rs = bufs
        settle(r_ref.at[pl.ds(0, 2), :, part_cols(n)], rs.at[n, 1])
        for h in range(2):
            col = half_cols(n, h)
            total = s_ref[x, :, col].astype(jnp.float32)
            for i in range(2):
                total = total + r_ref[i, :, col].astype(jnp.float32)
            updated = lat[lat_rows, col].astype(jnp.float32) - gate_row[:, col] * total
            write(col, updated.astype(jnp.bfloat16))

    bufs0 = (s0, r0, x0_ss.at[0], x0_rs)
    bufs1 = [(s1.at[k], r1.at[k], x1_ss.at[k], x1_rs.at[k]) for k in range(CHUNKS)]

    for copy in loads[5:]:
        copy.wait()
    w_send.wait_recv()
    o0_own.wait()
    o0_twin.wait_recv()
    project(a0, bufs0, 64)

    relay(1)
    send_kv((2, 3))
    send_q(0)
    pass_on(0)
    pass_on(1)
    send_q(1)
    pass_on(2)
    add_on(bufs0)
    relay(2)
    pass_on(3)

    oldest = position == 0

    def write_u0(col, updated):
        u0[:, col] = jnp.where(oldest, updated, jnp.zeros_like(updated))

    def finish0(n, carry):
        gather_x(bufs0, n, slice(None), write_u0)
        return carry

    y_width = D // NY

    def y_send(dy):
        to_y = lax.rem(y + dy, NY)
        return remote(
            u0.at[:, pl.ds(pl.multiple_of(to_y * y_width, 128), y_width)], ry.at[3 - dy],
            y_ss.at[0], y_rs.at[0], at(to_y, z, x, c),
        )

    def finish_released():
        lax.fori_loop(0, PARTS, finish0, 0)
        for dy in range(1, NY):
            y_send(dy).start()

    def z_window(zz):
        return pl.ds(pl.multiple_of((zz * 160 // 128) * 128, 128), 256)

    def z_send(dz):
        to_z = lax.rem(z + dz, NZ)
        return remote(
            u1.at[:, z_window(to_z)], rz.at[7 - dz], z_ss.at[0], z_rs.at[0],
            at(y, to_z, x, c),
        )

    def share_y():
        settle(ry, y_rs.at[0])
        total = u0[:, pl.ds(pl.multiple_of(y * y_width, 128), y_width)].astype(jnp.float32)
        for i in range(3):
            total = total + ry[i].astype(jnp.float32)
        u1[...] = total.astype(jnp.bfloat16)
        for dz in range(1, NZ):
            z_send(dz).start()

    def share_z():
        settle(rz, z_rs.at[0])
        total = u1[:, z_window(z)].astype(jnp.float32)
        for i in range(7):
            total = total + rz[i].astype(jnp.float32)
        turned = pltpu.roll(total, lax.rem(256 - (z % 4) * 32, 256), 1)
        rel_ref[...] = turned[:, :160].astype(jnp.bfloat16)

    settle(kv.at[23], load_sem.at[3])
    settle(qd.at[:, pl.ds(8, 2)], load_sem.at[4])
    settle(bias_all.at[pl.ds(0, NZ)], b_rs.at[0])
    settle(kv.at[pl.ds(NZ, NZ), :, other], ft_rs.at[0])

    def item(it):
        stays = (it >= FIRST_STAY) & (it < FIRST_STAY + 4)
        order = jnp.where(it < FIRST_STAY, it, it - 4)
        k = jnp.where(stays, (it - FIRST_STAY) // 2, order // 8)
        gathered_s = 7 - order % 8
        s = jnp.where(stays, 8 + it % 2, gathered_s)
        return k, s, s, jnp.where(stays, 16, s + 1)

    def o_send(it):
        k, j, s, _ = item(it)
        gathered = j < 8
        to_z = jnp.where(gathered, s, z)
        to_c = jnp.where(gathered, c, j - 8)
        head_col = jnp.where(gathered, (z // 4) * WIDTH + (z % 4) * HD, c * WIDTH + 4 * HD)
        dst = a1.at[k, :, :, pl.ds(pl.multiple_of(head_col, 128), 128)]
        rs = o_rs.at[k]
        return os.at[k, s], dst, o_ss.at[0], rs, to_z, to_c

    def arrived(it):
        k, j, s, _ = item(it)
        pl.when(it == FIRST_STAY)(lambda: relay(4))

        @pl.when(j < 8)
        def _():
            settle(qd.at[k, s], q_rs.at[k, s])

        @pl.when((0 < s) & (s < 8) & (k == 0))
        def _():
            pass_prev(s)

        @pl.when((s < 7) & (k == 0))
        def _():
            prev_to_twin(s + 1).wait_recv()

    def first_pass(q, s, base, i, sc, top):
        scores = lax.dot_general(q, kv[base + i, 0], NT, preferred_element_type=jnp.float32)
        sc[i] = scores
        return jnp.maximum(top, fold_max(scores) * SCALE2 + bias_all[s, 7 - i : 8 - i, :])

    def second_pass(s, base, i, sc, top, total, acc):
        p = jnp.exp2(sc[i] * SCALE2 - lanes(top - bias_all[s, 7 - i : 8 - i, :], 512))
        acc = acc + jnp.dot(
            p.astype(jnp.bfloat16), kv[base + i, 1], preferred_element_type=jnp.float32
        )
        return total + fold_sum(p), acc

    def row_top(top):
        return jnp.broadcast_to(jnp.max(top, axis=1, keepdims=True), (M, HD))

    def stage(it, sc, m_ref, next_sc, next_m, last=False):
        k, j, s, base = item(it)
        if not last:
            arrived(it + 1)
            k2, _, s2, base2 = item(it + 1)
            q = qd[k2, s2].reshape(M, HD)
        top = m_ref[...]
        next_top = jnp.full((M, HD), FAR, jnp.float32)
        total = jnp.zeros((M, HD), jnp.float32)
        acc = jnp.zeros((M, HD), jnp.float32)
        for i in range(8):
            if not last:
                next_top = first_pass(q, s2, base2, i, next_sc, next_top)
            total, acc = second_pass(s, base, i, sc, top, total, acc)
        if not last:
            next_m[...] = row_top(next_top)
        o = acc / jnp.sum(total, axis=1, keepdims=True)
        os[k, s] = o.astype(jnp.bfloat16).reshape(NX, CROWS, HD)
        src, dst, ss, rs, to_z, to_c = o_send(it)
        mine = (to_z == z) & (to_c == c)

        @pl.when(mine)
        def _():
            pltpu.make_async_copy(src, dst, rs).start()

        @pl.when(jnp.logical_not(mine))
        def _():
            remote(src, dst, ss, rs, at(y, to_z, x, to_c)).start()

    def project_chunk(k):
        settle(a1.at[k], o_rs.at[k])
        project(a1.at[k], bufs1[k], CROWS)

    arrived(0)
    k, _, s, base = item(0)
    q = qd[k, s].reshape(M, HD)
    top = jnp.full((M, HD), FAR, jnp.float32)
    for i in range(8):
        top = first_pass(q, s, base, i, sca, top)
    ma[...] = row_top(top)

    steps = {
        "r1": lambda: relay(1), "r2": lambda: relay(2), "r3": lambda: relay(3),
        "r4": lambda: relay(4), "q1": lambda: send_q(1), "fr": finish_released,
        "sy": share_y, "sz": share_z, "p0": lambda: project_chunk(0),
    }

    def run(todo):
        for name in todo:
            steps[name]()

    def pair(j, carry):
        stage(2 * j, sca, ma, scb, mb)

        @pl.when(j < N_ITEMS // 2 - 1)
        def _():
            stage(2 * j + 1, scb, mb, sca, ma)

        for at_j, todo in PLAN.items():
            pl.when(j == at_j)(functools.partial(run, todo))

        return carry

    lax.fori_loop(0, N_ITEMS // 2, pair, 0)
    stage(N_ITEMS - 1, scb, mb, sca, ma, last=True)
    add_on(bufs1[0])
    project_chunk(1)
    share_y()
    add_on(bufs1[1])

    def out_copy(k, n):
        rows = pl.ds(CROWS * k, CROWS)
        return pltpu.make_async_copy(
            new.at[rows, part_cols(n)], out_ref.at[rows, part_cols(n)], out_sem.at[0]
        )

    def finish(k):
        rows = pl.ds(CROWS * k, CROWS)

        def write(col, updated):
            new[rows, col] = jnp.where(oldest, fre[rows, col], updated)

        def part(n, carry):
            gather_x(bufs1[k], n, rows, write)
            out_copy(k, n).start()
            return carry

        lax.fori_loop(0, PARTS, part, 0)

    finish(0)
    finish(1)
    share_z()
    pltpu.make_async_copy(new, out_ref, out_sem.at[0]).wait()

    def drain():
        has_own = z // 4 == c

        @pl.when(has_own)
        def _():
            settle(kv.at[pl.ds(0, 7), 0], kv_ss.at[0])
            settle(qd.at[:, pl.ds(0, 7)], q_ss.at[0])
            settle(bias_all.at[pl.ds(0, 7)], b_ss.at[0])

        @pl.when(jnp.logical_not(has_own))
        def _():
            settle(kv.at[pl.ds(0, 8), 0], kv_ss.at[0])
            settle(qd.at[:, pl.ds(0, 8)], q_ss.at[0])
            settle(bias_all.at[pl.ds(0, 8)], b_ss.at[0])

        settle(kv.at[pl.ds(0, 7)], rel_ss.at[0])
        w_send.wait_send()
        o0_twin.wait_send()
        settle(kv.at[pl.ds(0, 8), :, half], ft_ss.at[0])
        settle(kv.at[pl.ds(0, 7), :, half], fy_ss.at[0])
        settle(kv.at[pl.ds(0, 7), :, half], fty_ss.at[0])
        for bufs in [bufs0] + bufs1:
            settle(bufs[1], bufs[2])
        settle(ry, y_ss.at[0])
        settle(rz, z_ss.at[0])
        settle(os.at[:, pl.ds(0, 8)], o_ss.at[0])

    drain()


def body(
    latent, queries, keys, values, out_weight, level_gate, levels, offset, lag_mask, fresh_noise
):
    bf16, f32 = jnp.bfloat16, jnp.float32
    hbm = pl.BlockSpec(memory_space=pl.ANY)
    vmem = pl.BlockSpec(memory_space=pltpu.VMEM)
    smem = pl.BlockSpec(memory_space=pltpu.SMEM)
    dma = pltpu.SemaphoreType.DMA
    vm = pltpu.VMEM
    scratch = [
        vm((2 * WIDTH, D), bf16),
        vm((24, 2, ROWS, HD), bf16),
        vm((CHUNKS, ITEMS, NX, CROWS, HD), bf16),
        vm((ITEMS, 8, 128), f32),
        vm((CHUNKS, ITEMS, NX, CROWS, HD), bf16),
        vm((CHUNKS, NX, CROWS, 2 * WIDTH), bf16),
        vm((NX, 2, 64, WIDTH), bf16),
        vm((ROWS, WIDTH), bf16),
        vm((ROWS, WIDTH), bf16),
        vm((NX, 2, 64, WIDTH), bf16),
        vm((NX, 64, 2 * WIDTH), bf16),
        vm((NX, 64, D), bf16),
        vm((NX - 1, 64, D), bf16),
        vm((CHUNKS, NX, CROWS, D), bf16),
        vm((CHUNKS, NX - 1, CROWS, D), bf16),
        vm((64, D), bf16),
        vm((NY - 1, 64, D // NY), bf16),
        vm((64, D // NY), bf16),
        vm((NZ - 1, 64, 256), bf16),
        vm((64, D), bf16),
        vm((64, D), bf16),
        vm((64, D), bf16),
        vm((1, D), f32),
        vm((8, 128), f32),
        vm((8, M, ROWS), f32),
        vm((8, M, ROWS), f32),
        vm((M, HD), f32),
        vm((M, HD), f32),
        dma((8,)),
        dma((1,)), dma((NZ,)),
        dma((1,)), dma((2, 4)),
        dma((1,)), dma((CHUNKS, NZ)),
        dma((1,)), dma((1,)),
        dma((1,)), dma((1,)),
        dma((1,)), dma((1,)),
        dma((1,)), dma((NZ,)),
        dma((1,)), dma((NZ,)),
        dma((3,)),
        dma((1,)), dma((PARTS, 2)),
        dma((1,)), dma((CHUNKS,)),
        dma((CHUNKS,)), dma((CHUNKS, PARTS, 2)),
        dma((1,)),
        dma((1,)), dma((1,)),
        dma((1,)), dma((1,)),
    ]
    return pl.pallas_call(
        kernel,
        out_shape=(
            jax.ShapeDtypeStruct((64, D), bf16),
            jax.ShapeDtypeStruct((64, 160), bf16),
        ),
        in_specs=[hbm, hbm, hbm, hbm, hbm, vmem, smem, smem, smem, hbm],
        out_specs=(hbm, vmem),
        scratch_shapes=scratch,
        compiler_params=pltpu.CompilerParams(
            collective_id=1, has_side_effects=True, vmem_limit_bytes=56 << 20
        ),
        name="window_step",
    )(
        latent, queries.reshape(NX, 2, 64, WIDTH), keys, values, out_weight, level_gate,
        levels, offset, lag_mask, fresh_noise,
    )


def solution(mesh):
    return jax.shard_map(
        body,
        mesh=mesh,
        in_specs=(
            P(("span", "tp"), None),
            P("span", "tp"),
            P("span", "tp"),
            P("span", "tp"),
            P("tp", None),
            P(),
            P("span"),
            P(),
            P("span", None),
            P("tp", None),
        ),
        out_specs=(P(("span", "tp"), None), P("tp", "span")),
        check_vma=False,
    )
```

time: 143 us -> 117 us (0.82)
  Pallas kernels: 135 us -> 110 us
    pallas_call x1, Pallas kernels: 135 us -> 110 us  [body(): pl.pallas_call(kernel, out_shape=(jax.ShapeDtypeStruct((64, D), bf16), ja...]
where the time goes in v2:
time: 117 us; the launch traced here: 116 us
  Pallas kernels  110 us (94%)
  local copies, waits for them, and re-layouts  3.34 us (3%)
  between operations  1.93 us (2%)
    pallas_call x1, Pallas kernels, body(): pl.pallas_call(kernel, out_shape=(jax.ShapeDtypeStruct((64, D), bf16), ja...  110 us
    unnamed x2, local copies, waits for them, and re-layouts  3.34 us

profile of v2, /device:TPU:2, one launch (start us, length us, event | category | flops | bytes accessed | tf_op | source)
XLA Modules:
  0.0 115.6 jit_solution(6831878366111614129)
XLA Ops:
  1.9 110.3 %window_step.1 = (bf16[64,5120]{1,0:T(8,128)(2,1)}, bf16[64,160]{1,0:T(8,128)(2,1)}) custom-call(bf16[64,5120]{1,0:T(8,128)(2,1)} %latent_ref.1, bf16[4,2,64,640]{3,2,1,0:T(8,128)(2,1)} %bitcast.1, bf16[512,640]{1,0:T(8,128)(2,1)} %k_ref.1, bf16[512,640]{1,0:T(8,128)(2,1)} %v_ref.1, bf16[640,5120]{1,0:T(8,128)(2,1)} %w_ref.1, f32[4,5120]{1,0:T(4,128)} %gate_ref.1, ...), custom_call_target="tpu_custom_call" | custom-call | tf_op jit(solution)/shard_map/window_step/pallas_call | solution.py:641
  112.3 2.0 %copy.16 = bf16[64,5120]{1,0:T(8,128)(2,1)} copy(bf16[64,5120]{1,0:T(8,128)(2,1)} %get-tuple-element.4) | data formatting | bytes 1310720
  114.2 1.4 %copy.17 = bf16[64,160]{1,0:T(8,128)(2,1)} copy(bf16[64,160]{1,0:T(8,128)(2,1)} %get-tuple-element.5) | data formatting | bytes 40960

commit v3 on v2

--- a/solution.py
+++ b/solution.py
@@ -25,8 +25,8 @@
 COLS = 1024
 PARTS = D // COLS
 NT = (((1,), (1,)), ((), ()))
-FIRST_STAY = 12
-PLAN = {1: ("r3",), 5: ("fr",), 7: ("p0",)}
+FIRST_STAY = 14
+PLAN = {1: ("r3",), 5: ("fr",), 8: ("p0",)}
 
 
 def lanes(col, width):
@@ -581,6 +581,11 @@
         settle(os.at[:, pl.ds(0, 8)], o_ss.at[0])
 
     drain()
+
+
+def hand_over(next_in, rel_in, next_out, rel_out):
+    next_out[...] = next_in[...]
+    rel_out[...] = rel_in[...]
 
 
 def body(
@@ -638,7 +643,7 @@
         dma((1,)), dma((1,)),
         dma((1,)), dma((1,)),
     ]
-    return pl.pallas_call(
+    made = pl.pallas_call(
         kernel,
         out_shape=(
             jax.ShapeDtypeStruct((64, D), bf16),
@@ -655,6 +660,13 @@
         latent, queries.reshape(NX, 2, 64, WIDTH), keys, values, out_weight, level_gate,
         levels, offset, lag_mask, fresh_noise,
     )
+    return pl.pallas_call(
+        hand_over,
+        out_shape=tuple(jax.ShapeDtypeStruct(a.shape, a.dtype) for a in made),
+        in_specs=[vmem, vmem],
+        out_specs=(vmem, vmem),
+        name="hand_over",
+    )(*made)
 
 
 def solution(mesh):

time: 117 us -> 114 us (0.974)
  local copies, waits for them, and re-layouts: 3.34 us -> 0 us
    unnamed x2 -> x0, local copies, waits for them, and re-layouts: 3.34 us -> none
    pallas_call x0 -> x1, Pallas kernels: none -> 1.97 us  [body(): pl.pallas_call(hand_over, out_shape=tuple((jax.ShapeDtypeStruct(a.shape,...]
    pallas_call x1, Pallas kernels: 110 us -> 109 us  [body(): pl.pallas_call(kernel, out_shape=(jax.ShapeDtypeStruct((64, D), bf16), ja...]
where the time goes in v3:
time: 114 us; the launch traced here: 113 us
  Pallas kernels  111 us (97%)
  between operations  1.93 us (2%)
    pallas_call x1, Pallas kernels, body(): pl.pallas_call(kernel, out_shape=(jax.ShapeDtypeStruct((64, D), bf16), ja...  109 us

profile of v3, /device:TPU:2, one launch (start us, length us, event | category | flops | bytes accessed | tf_op | source)
XLA Modules:
  0.0 112.7 jit_solution(7123334584961188252)
XLA Ops:
  1.9 108.8 %window_step.1 = (bf16[64,5120]{1,0:T(8,128)(2,1)}, bf16[64,160]{1,0:T(8,128)(2,1)}) custom-call(bf16[64,5120]{1,0:T(8,128)(2,1)} %latent_ref.1, bf16[4,2,64,640]{3,2,1,0:T(8,128)(2,1)} %bitcast.1, bf16[512,640]{1,0:T(8,128)(2,1)} %k_ref.1, bf16[512,640]{1,0:T(8,128)(2,1)} %v_ref.1, bf16[640,5120]{1,0:T(8,128)(2,1)} %w_ref.1, f32[4,5120]{1,0:T(4,128)} %gate_ref.1, ...), custom_call_target="tpu_custom_call" | custom-call | tf_op jit(solution)/shard_map/window_step/pallas_call | solution.py:646
  110.7 2.0 %hand_over.1 = (bf16[64,5120]{1,0:T(8,128)(2,1)}, bf16[64,160]{1,0:T(8,128)(2,1)}) custom-call(bf16[64,5120]{1,0:T(8,128)(2,1)} %get-tuple-element.4.next_in, bf16[64,160]{1,0:T(8,128)(2,1)} %get-tuple-element.5.rel_in), custom_call_target="tpu_custom_call" | custom-call | tf_op jit(solution)/shard_map/hand_over/pallas_call | solution.py:663
